TPU v7x, 32 devices: a whole 2x2x4 slice. The times are simulated.
32 devices in a mesh: span: 4 (over y, x), tile: 8 (over z, core).
Axes of the slice: x: 2, y: 2, z: 4, core: 2. Of those that a mesh axis runs over, the one named last changes fastest.
Arguments:
- clean_latents: bfloat16 [4, 2, 32, 2560], P('span', None, 'tile'), may hold values from -6 to 6
- noise_draws: bfloat16 [4, 2, 32, 2560], P('span', None, 'tile'), may hold values from -6 to 6
- noise_level: float32 [4], P('span'), may hold values from 0.3 to 3
- memory_bank: bfloat16 [128, 32, 2560], P('span', 'tile'), may hold values from -6 to 6
- memory_index: int32 [4, 16], P('span'), may hold values from 0 to 127, as said below
- stem_weight: bfloat16 [16, 512], replicated, may hold values from -1.5 to 1.5
- memory_weight: bfloat16 [256, 512], replicated, may hold values from -0.375 to 0.375
- conv_weight: bfloat16 [2, 3, 3, 3, 32, 512], replicated, may hold values from -0.21875 to 0.21875
- norm_gain: float32 [2, 512], replicated, may hold values from 0.1 to 1.9
- head_weight: bfloat16 [512, 16], replicated, may hold values from -0.25 to 0.25
Outputs:
- prediction: bfloat16 [4, 2, 32, 2560], P('span', None, 'tile')
Inputs may be any that keep to these rules, and one draw needn't show every extreme that they name: `memory_index`: entry = owner span times 32 plus a frame of that owner. No row names more than 4 entries of one owner; one owner, the same for all rows, is named exactly 4 times in every row. Entries may repeat.
All inputs are finite; a program needn't handle non-finite values.
Results may differ from a plain program's by a relative error of at most 0.012.
Values may be sent and summed in bfloat16 or wider, within the bound.
A program may use at most 128 MiB of HBM per device.

v0:
```python
import jax
import jax.numpy as jnp
from jax import lax
from jax.sharding import PartitionSpec as P

CTX = 2
CAP = 4


def shifted(value, axis, steps):
    count = lax.axis_size(axis)
    first, last = (max(0, -steps), min(count, count - steps))
    return lax.ppermute(value, axis, [(source, source + steps) for source in range(first, last)])


def with_halo(block, sides, width):
    for axis, dim in sides:
        count = lax.axis_size(axis)
        forward = [(i, i + 1) for i in range(count - 1)]
        backward = [(target, source) for source, target in forward]
        low = lax.ppermute(
            lax.slice_in_dim(block, block.shape[dim] - width, None, axis=dim), axis, forward
        )
        high = lax.ppermute(lax.slice_in_dim(block, 0, width, axis=dim), axis, backward)
        block = jnp.concatenate([low, block, high], axis=dim)
    return block


def normed_silu(hidden, gain_row):
    values = hidden.astype(jnp.float32)
    mean_square = jnp.mean(values * values, axis=-1, keepdims=True)
    scaled = values * lax.rsqrt(mean_square + 1e-06) * gain_row
    return jax.nn.silu(scaled).astype(jnp.bfloat16)


def causal_conv(active, weight):
    frames, rows_in, col_count, channels = active.shape
    group_width = weight.shape[3]
    group_count = channels // group_width
    rows_out = rows_in - 2
    padded = jnp.pad(active, ((2, 0), (0, 0), (1, 1), (0, 0)))
    padded = padded.reshape(frames + 2, rows_in, col_count + 2, group_count, group_width)
    kernels = weight.reshape(3, 3, 3 * group_width, group_count, group_width)

    def one_frame(frame_number):
        window_frames = lax.dynamic_slice_in_dim(padded, frame_number, 3, 0)
        accumulated = jnp.zeros((rows_out, col_count, group_count, group_width), jnp.float32)
        for time_tap in range(3):
            for row_tap in range(3):
                plane = window_frames[time_tap, row_tap : row_tap + rows_out]
                joined = jnp.concatenate(
                    [plane[:, col_tap : col_tap + col_count] for col_tap in range(3)], axis=-1
                )
                accumulated = accumulated + jnp.einsum(
                    "hwgi,igo->hwgo",
                    joined,
                    kernels[time_tap, row_tap],
                    preferred_element_type=jnp.float32,
                )
        return accumulated

    result = lax.map(one_frame, jnp.arange(frames, dtype=jnp.int32))
    return result.reshape(frames, rows_out, col_count, channels)


def embed_frames(sequence, memory, stem_weight, memory_weight):
    latent_width, channels = stem_weight.shape
    frames, row_count, merged = sequence.shape
    col_count = merged // latent_width
    memory_count = memory.shape[0]
    stem_term = jnp.dot(
        sequence.reshape(frames * row_count * col_count, latent_width),
        stem_weight,
        preferred_element_type=jnp.float32,
    ).reshape(frames, row_count, col_count, channels)
    stacked = jnp.transpose(
        memory.reshape(memory_count, row_count, col_count, latent_width), (1, 2, 0, 3)
    ).reshape(row_count * col_count, memory_count * latent_width)
    memory_term = jnp.dot(stacked, memory_weight, preferred_element_type=jnp.float32).reshape(
        row_count, col_count, channels
    )
    return (stem_term + memory_term[None]).astype(jnp.bfloat16)


def fetch_memory(memory_bank, memory_index):
    wanted = memory_index[0]
    bank_frames, row_count, merged = memory_bank.shape
    span_count = lax.axis_size("span")
    memory_count = wanted.shape[0]
    owner_span = wanted // bank_frames
    local_frame = wanted % bank_frames
    positions = jnp.arange(memory_count, dtype=jnp.int32)
    same_owner = (owner_span[:, None] == owner_span[None, :]) & (
        positions[None, :] < positions[:, None]
    )
    owner_rank = jnp.sum(same_owner.astype(jnp.int32), axis=1)
    reply_slot = owner_span * CAP + owner_rank
    slot_match = jnp.arange(span_count * CAP, dtype=jnp.int32)[:, None] == reply_slot[None, :]
    request = jnp.sum(jnp.where(slot_match, local_frame[None, :] + 1, 0), axis=1) - 1
    request = request.reshape(span_count, CAP)
    incoming = lax.all_to_all(request, "span", split_axis=0, concat_axis=0, tiled=True)
    picked = memory_bank[jnp.maximum(incoming, 0).reshape(-1)].reshape(
        span_count, CAP, row_count, merged
    )
    returned = lax.all_to_all(picked, "span", split_axis=0, concat_axis=0, tiled=True)
    return returned.reshape(span_count * CAP, row_count, merged)[reply_slot]


def shards(
    clean_latents,
    noise_draws,
    noise_level,
    memory_bank,
    memory_index,
    stem_weight,
    memory_weight,
    conv_weight,
    norm_gain,
    head_weight,
):
    channels = stem_weight.shape[1]
    frames = clean_latents.shape[1]
    row_count = clean_latents.shape[2]
    merged = clean_latents.shape[3]
    layer_total = conv_weight.shape[0]
    noise_sigma = noise_level[0]
    noisy = (
        (clean_latents[0].astype(jnp.float32) + noise_sigma * noise_draws[0].astype(jnp.float32))
        * lax.rsqrt(1.0 + noise_sigma * noise_sigma)
    ).astype(jnp.bfloat16)
    previous = shifted(clean_latents[0, frames - CTX :], "span", 1)
    memory = fetch_memory(memory_bank, memory_index)
    sequence = jnp.concatenate([previous, noisy], axis=0)
    hidden = embed_frames(sequence, memory, stem_weight, memory_weight)
    for layer_number in range(layer_total):
        active = normed_silu(hidden, norm_gain[layer_number])
        extended = with_halo(active, (("tile", 1),), 1)
        update = causal_conv(extended, conv_weight[layer_number])
        hidden = (hidden.astype(jnp.float32) + update).astype(jnp.bfloat16)
    tail = hidden[CTX:].reshape(-1, channels)
    output = jnp.dot(tail, head_weight, preferred_element_type=jnp.float32).astype(jnp.bfloat16)
    return output.reshape(1, frames, row_count, merged)


def solution(mesh):
    return jax.shard_map(
        shards,
        mesh=mesh,
        in_specs=(
            P("span", None, "tile", None),
            P("span", None, "tile", None),
            P("span"),
            P("span", "tile", None),
            P("span", None),
            P(),
            P(),
            P(),
            P(),
            P(),
        ),
        out_specs=P("span", None, "tile", None),
        check_vma=False,
    )
```

profile of v0, /device:TPU:1, one launch (start us, length us, event | category | flops | bytes accessed | tf_op | source)
XLA Modules:
  0.0 1017.8 jit_solution(1245328577182472470)
XLA Ops:
  32.6 5.8 collective-permute-start.1
  41.7 5.0 reshape_squeeze.6
  46.7 5.1 copy.69
  55.0 7.7 copy.107
  62.7 9.3 pad.7.clone
  76.3 437.9 %while.20 = (s32[]{:T(128)}, f32[4,4,160,16,32]{2,4,3,1,0:T(8,128)}, s32[4]{0:T(128)S(1)}, bf16[6,6,162,16,32]{2,4,3,1,0:T(8,128)(2,1)}, bf16[3,3,96,16,32]{2,4,...) while((s32[]{:T(128)}, f32[4,4,160,16,32]{2,4,3,1,0:T(8,128)}, s32[4]{0:T(128)S(1)}, ...), condition=%wide.region_4.5_spmd, body=%wide.region_3.4_spmd.sunk | while | flops 621936640 | bytes 119046928 | solution.py:62
  100.5 7.5 constant_dynamic-slice_fusion.20
  133.2 4.7 fusion.315
  182.9 4.7 fusion.303
  193.3 6.3 add_bitcast_fusion.4
  203.4 7.5 constant_dynamic-slice_fusion.20
  236.1 4.7 fusion.315
  285.9 4.7 fusion.303
  296.3 6.3 add_bitcast_fusion.4
  306.4 7.3 constant_dynamic-slice_fusion.20
  339.0 4.7 fusion.315
  388.7 4.7 fusion.303
  399.1 6.3 add_bitcast_fusion.4
  409.2 7.5 constant_dynamic-slice_fusion.20
  441.8 4.7 fusion.315
  491.6 4.7 fusion.303
  502.0 6.3 add_bitcast_fusion.4
  514.3 9.0 copy.71
  535.4 5.0 reshape_squeeze.7
  540.4 5.1 copy.74
  548.7 7.7 copy.108
  556.4 9.3 pad.8.clone
  570.1 435.5 %while.21 = (s32[]{:T(128)}, f32[4,4,160,16,32]{2,4,3,1,0:T(8,128)}, s32[4]{0:T(128)S(1)}, bf16[6,6,162,16,32]{2,4,3,1,0:T(8,128)(2,1)}, bf16[3,3,96,16,32]{2,4,...) while((s32[]{:T(128)}, f32[4,4,160,16,32]{2,4,3,1,0:T(8,128)}, s32[4]{0:T(128)S(1)}, ...), condition=%wide.region_7.8_spmd, body=%wide.region_6.7_spmd.sunk | while | flops 621936640 | bytes 119046928 | solution.py:62
  595.4 7.6 constant_dynamic-slice_fusion.21
  608.3 4.8 fusion.346
  618.3 4.7 fusion.348
  628.3 4.7 fusion.350
  688.3 6.3 add_bitcast_fusion.5
  698.6 7.6 constant_dynamic-slice_fusion.21
  711.5 4.8 fusion.346
  721.5 4.7 fusion.348
  731.5 4.7 fusion.350
  791.6 6.3 add_bitcast_fusion.5
  801.9 7.4 constant_dynamic-slice_fusion.21
  814.6 4.8 fusion.346
  824.6 4.7 fusion.348
  834.6 4.7 fusion.350
  894.6 6.3 add_bitcast_fusion.5
  904.9 7.5 constant_dynamic-slice_fusion.21
  917.7 4.8 fusion.346
  927.7 4.7 fusion.348
  937.7 4.7 fusion.350
  997.8 6.3 add_bitcast_fusion.5
  (312 shorter events, 677.6 us)
Async XLA Ops:
  0.0 13.7 %copy-start = (bf16[32,4,2560]{2,1,0:T(4,128)(2,1)S(1)}, bf16[32,4,2560]{2,1,0:T(4,128)(2,1)}, u32[]{:S(2)}) copy-start(bf16[32,4,2560]{2,1,0:T(4,128)(2,1)} %param.17) | copy-start | bytes 1966084
  2.4 11.2 %all-to-all-start = ((s32[4,1,4]{2,1,0:T(1,128)}), s32[4,1,4]{2,1,0:T(1,128)S(1)}, u32[]{:S(2)}, u32[]{:S(2)}) async-start(s32[4,1,4]{2,1,0:T(1,128)} %bitcast.88), calls=%async_computation | async-start | bytes 4096 | tf_op jit(solution)/shard_map/all_to_all | solution.py:101
  6.6 12.1 %collective-permute-start = (bf16[2,4,2560]{2,1,0:T(4,128)(2,1)}, bf16[2,4,2560]{2,1,0:T(4,128)(2,1)S(1)}, u32[]{:S(2)}, u32[]{:S(2)}) collective-permute-start(bf16[2,4,2560]{2,1,0:T(4,128)(2,1)} %bitcast.337), channel_id=1, source_target_pairs={{0,8},{8,16},{16,24},{1,9},{9,17},{17,25},{2,10},{10,18},{18,26},{... | collective-permute-start | bytes 122888 | tf_op jit(solution)/shard_map/ppermute | solution.py:13
  15.3 7.8 all-to-all-start.1
  24.0 3.5 copy-start.10
  26.1 1.7 copy-start.13
  29.9 1.7 copy-start.7
  31.6 8.7 copy-start.9
  32.6 19.2 %collective-permute-start.1 = (bf16[4,1,160,512]{3,2,1,0:T(8,128)(2,1)}, bf16[4,1,160,512]{3,2,1,0:T(8,128)(2,1)}, u32[]{:S(2)}, u32[]{:S(2)}) collective-permute-start(bf16[4,1,160,512]{3,2,1,0:T(8,128)(2,1)} %get-tuple-element.207), channel_id=1, source_target_pairs={{0,1},{1,2},{2,3},{3,4},{4,5},{5,6},{6,7},{8,9},{9,10},{10,11},{11... | collective-permute-start | bytes 1966088 | tf_op jit(solution)/shard_map/ppermute | solution.py:21
  38.4 13.4 %collective-permute-start.2 = (bf16[4,1,160,512]{3,2,1,0:T(8,128)(2,1)S(1)}, bf16[4,1,160,512]{3,2,1,0:T(8,128)(2,1)}, u32[]{:S(2)}, u32[]{:S(2)}) collective-permute-start(bf16[4,1,160,512]{3,2,1,0:T(8,128)(2,1)S(1)} %get-tuple-element.208), channel_id=1, source_target_pairs={{1,0},{2,1},{3,2},{4,3},{5,4},{6,5},{7,6},{9,8},{10,9},{11,10},{12... | collective-permute-start | bytes 1966088 | tf_op jit(solution)/shard_map/ppermute | solution.py:24
  191.1 1.8 copy-start.2
  191.1 2.2 copy-start.4
  294.1 1.8 copy-start.2
  294.1 2.2 copy-start.4
  396.9 1.8 copy-start.2
  396.9 2.2 copy-start.4
  499.8 1.8 copy-start.2
  499.8 2.2 copy-start.4
  514.2 9.0 copy-start.8
  523.3 3.3 copy-start.12
  526.6 2.3 copy-start.6
  529.9 15.7 %collective-permute-start.3 = (bf16[4,1,160,512]{3,2,1,0:T(8,128)(2,1)}, bf16[4,1,160,512]{3,2,1,0:T(8,128)(2,1)}, u32[]{:S(2)}, u32[]{:S(2)}) collective-permute-start(bf16[4,1,160,512]{3,2,1,0:T(8,128)(2,1)} %get-tuple-element.205), channel_id=1, source_target_pairs={{0,1},{1,2},{2,3},{3,4},{4,5},{5,6},{6,7},{8,9},{9,10},{10,11},{11... | collective-permute-start | bytes 1966088 | tf_op jit(solution)/shard_map/ppermute | solution.py:21
  533.5 12.0 %collective-permute-start.4 = (bf16[4,1,160,512]{3,2,1,0:T(8,128)(2,1)S(1)}, bf16[4,1,160,512]{3,2,1,0:T(8,128)(2,1)}, u32[]{:S(2)}, u32[]{:S(2)}) collective-permute-start(bf16[4,1,160,512]{3,2,1,0:T(8,128)(2,1)S(1)} %get-tuple-element.206), channel_id=1, source_target_pairs={{1,0},{2,1},{3,2},{4,3},{5,4},{6,5},{7,6},{9,8},{10,9},{11,10},{12... | collective-permute-start | bytes 1966088 | tf_op jit(solution)/shard_map/ppermute | solution.py:24
  686.1 1.8 copy-start.3
  686.1 2.2 copy-start.5
  789.3 1.8 copy-start.3
  789.3 2.2 copy-start.5
  892.4 1.8 copy-start.3
  892.4 2.2 copy-start.5
  995.6 1.8 copy-start.3
  995.6 2.2 copy-start.5
  1013.5 2.3 copy-start.11
  1013.5 3.9 copy-start.1
where the time goes:
time: 1030 us; the launch traced here: 1020 us
  local copies, waits for them, and re-layouts  552 us (54%)
  matrix products  354 us (34%)
  loops' own time  65.1 us (6%)
  starting transfers between devices  24.3 us (2%)
  other arithmetic  18.4 us (2%)
    dot_general x72, matrix products, one_frame(): jnp.einsum('hwgi,igo->hwgo', joined, kernels[time_tap, row_tap], preferre...  351 us
    while x104, local copies, waits for them, and re-layouts  251 us
    slice x72, local copies, waits for them, and re-layouts, one_frame(): plane[:, col_tap:col_tap + col_count]  130 us
    another operation x2, loops' own time, causal_conv(): result = lax.map(one_frame, jnp.arange(frames, dtype=jnp.int32))  65.1 us
    slice x8, local copies, waits for them, and re-layouts, one_frame(): plane = window_frames[time_tap, row_tap:row_tap + rows_out]  59.9 us
  transfers between devices with their start and end apart: 7, of which 1 were waited for; matrix products, arithmetic and copies ran while one was open for 3% of the time, Pallas kernels for 0%

commit v1 on v0

v1 whole, which is shorter than its diff:
```python
import functools

import jax
import jax.numpy as jnp
from jax import lax
from jax.experimental import pallas as pl
from jax.experimental.pallas import tpu as pltpu
from jax.sharding import PartitionSpec as P

CTX = 2
CAP = 4
BLK = 256
CHUNK = 2


def shifted(value, axis, steps):
    count = lax.axis_size(axis)
    first, last = (max(0, -steps), min(count, count - steps))
    return lax.ppermute(value, axis, [(source, source + steps) for source in range(first, last)])


def with_halo(block, sides, width):
    for axis, dim in sides:
        count = lax.axis_size(axis)
        forward = [(i, i + 1) for i in range(count - 1)]
        backward = [(target, source) for source, target in forward]
        low = lax.ppermute(
            lax.slice_in_dim(block, block.shape[dim] - width, None, axis=dim), axis, forward
        )
        high = lax.ppermute(lax.slice_in_dim(block, 0, width, axis=dim), axis, backward)
        block = jnp.concatenate([low, block, high], axis=dim)
    return block


def select_frames(frames, index):
    chosen = index[:, None] == jnp.arange(frames.shape[0], dtype=jnp.int32)[None, :]
    return jnp.einsum(
        "sf,frm->srm",
        chosen.astype(jnp.bfloat16),
        frames,
        preferred_element_type=jnp.float32,
    ).astype(jnp.bfloat16)


def fetch_memory(memory_bank, memory_index):
    wanted = memory_index[0]
    bank_frames, row_count, merged = memory_bank.shape
    span_count = lax.axis_size("span")
    memory_count = wanted.shape[0]
    owner_span = wanted // bank_frames
    local_frame = wanted % bank_frames
    positions = jnp.arange(memory_count, dtype=jnp.int32)
    same_owner = (owner_span[:, None] == owner_span[None, :]) & (
        positions[None, :] < positions[:, None]
    )
    owner_rank = jnp.sum(same_owner.astype(jnp.int32), axis=1)
    reply_slot = owner_span * CAP + owner_rank
    slot_match = jnp.arange(span_count * CAP, dtype=jnp.int32)[:, None] == reply_slot[None, :]
    request = jnp.sum(jnp.where(slot_match, local_frame[None, :] + 1, 0), axis=1) - 1
    request = request.reshape(span_count, CAP)
    incoming = lax.all_to_all(request, "span", split_axis=0, concat_axis=0, tiled=True)
    picked = select_frames(memory_bank, incoming.reshape(-1)).reshape(
        span_count, CAP, row_count, merged
    )
    returned = lax.all_to_all(picked, "span", split_axis=0, concat_axis=0, tiled=True)
    return select_frames(returned.reshape(span_count * CAP, row_count, merged), reply_slot)


def kernel(rows, x_ref, w_ref, cw_ref, gain_ref, head_ref, out_ref, h0, a1, h1, a2, wexp):
    frames = h0.shape[0]
    cols = x_ref.shape[0] // (rows + 4)
    tile = lax.axis_index("tile")
    total_rows = lax.axis_size("tile") * rows

    def activate(hidden, layer):
        values = hidden.astype(jnp.float32)
        scale = lax.rsqrt(jnp.mean(values * values, axis=-1, keepdims=True) + 1e-06)
        half = values * scale * (0.5 * gain_ref[layer : layer + 1, :])
        return half * (1.0 + jnp.tanh(half))

    @pl.loop(0, rows + 4)
    def _(row):
        at = pl.ds(pl.multiple_of(row * cols, 16), cols)
        stacked = x_ref[at, :]
        for frame in range(frames):
            hidden = jnp.dot(
                stacked, w_ref[frame], preferred_element_type=jnp.float32
            ).astype(jnp.bfloat16)
            h0[frame, at, :] = hidden
            a1[frame, at, :] = activate(hidden, 0).astype(jnp.bfloat16)

    in_group = lax.broadcasted_iota(jnp.int32, (BLK, BLK), 0) // 32
    out_group = lax.broadcasted_iota(jnp.int32, (BLK, BLK), 1) // 32
    diagonal = (in_group == out_group).astype(jnp.float32).astype(jnp.bfloat16)
    size = CHUNK * cols
    column = lax.rem(lax.broadcasted_iota(jnp.int32, (size, BLK), 0), cols)

    def conv(layer, source, base, first_frame, row_count, target):
        @pl.loop(0, 2)
        def _(half):
            lanes = pl.ds(pl.multiple_of(half * BLK, BLK), BLK)

            @pl.loop(0, 9)
            def _(tap):
                for dx in range(3):
                    narrow = cw_ref[layer, tap * 3 + dx, :, lanes]
                    wide = jnp.concatenate([narrow] * (BLK // 32), axis=0)
                    wexp[dx, pl.ds(pl.multiple_of(tap * BLK, BLK), BLK), :] = wide * diagonal

            def one_frame(frame, taps):
                @pl.loop(0, row_count // CHUNK)
                def _(chunk):
                    start = chunk * size
                    pieces = [
                        source[
                            frame + dt - 2,
                            pl.ds(pl.multiple_of(start + dy * cols, 16), size),
                            lanes,
                        ]
                        for dt in range(3 - taps, 3)
                        for dy in range(3)
                    ]
                    joined = jnp.concatenate(pieces, axis=1)
                    total = base[
                        frame, pl.ds(pl.multiple_of(start + cols, 16), size), lanes
                    ].astype(jnp.float32)
                    for dx in range(3):
                        term = jnp.dot(
                            joined,
                            wexp[dx, (3 - taps) * 3 * BLK :, :],
                            preferred_element_type=jnp.float32,
                        )
                        if dx == 0:
                            term = jnp.where(column == 0, 0.0, pltpu.roll(term, 1, 0))
                        if dx == 2:
                            term = jnp.where(
                                column == cols - 1, 0.0, pltpu.roll(term, size - 1, 0)
                            )
                        total = total + term
                    target[
                        frame - first_frame, pl.ds(pl.multiple_of(start, 16), size), lanes
                    ] = total.astype(jnp.bfloat16)

            for frame in range(first_frame, min(2, frames)):
                one_frame(frame, frame + 1)
            pl.loop(2, frames)(lambda frame: one_frame(frame, 3))

    conv(0, a1, h0, 0, rows + 2, h1)

    @pl.loop(0, rows + 2)
    def _(row):
        place = tile * rows + row - 1
        keep = ((place >= 0) & (place < total_rows)).astype(jnp.float32)
        at = pl.ds(pl.multiple_of(row * cols, 16), cols)
        for frame in range(frames):
            a2[frame, at, :] = (activate(h1[frame, at, :], 1) * keep).astype(jnp.bfloat16)

    conv(1, a2, h1, CTX, rows, h0)

    for frame in range(frames - CTX):
        out_ref[frame] = jnp.dot(
            h0[frame, : rows * cols, :], head_ref[...], preferred_element_type=jnp.float32
        ).astype(jnp.bfloat16)


def shards(
    clean_latents,
    noise_draws,
    noise_level,
    memory_bank,
    memory_index,
    stem_weight,
    memory_weight,
    conv_weight,
    norm_gain,
    head_weight,
):
    latent, channels = stem_weight.shape
    frames, rows, merged = clean_latents.shape[1:]
    cols = merged // latent
    sigma = noise_level[0]
    noisy = (
        (clean_latents[0].astype(jnp.float32) + sigma * noise_draws[0].astype(jnp.float32))
        * lax.rsqrt(1.0 + sigma * sigma)
    ).astype(jnp.bfloat16)
    previous = shifted(clean_latents[0, frames - CTX :], "span", 1)
    memory = fetch_memory(memory_bank, memory_index)
    stack = jnp.concatenate([memory, previous, noisy], axis=0)
    stack = with_halo(stack, (("tile", 1),), 2)
    depth = stack.shape[0] * latent
    wide = rows + 4
    stack = jnp.transpose(
        stack.reshape(stack.shape[0], wide, cols, latent), (1, 2, 0, 3)
    ).reshape(wide * cols, depth)
    count = CTX + frames
    weights = jnp.concatenate(
        [
            jnp.broadcast_to(memory_weight[None], (count,) + memory_weight.shape),
            (
                jnp.eye(count, dtype=jnp.bfloat16)[:, :, None, None] * stem_weight[None, None]
            ).reshape(count, count * latent, channels),
        ],
        axis=1,
    )
    taps = conv_weight.reshape(conv_weight.shape[0], 27, conv_weight.shape[4], channels)
    vmem = pl.BlockSpec(memory_space=pltpu.VMEM)
    output = pl.pallas_call(
        functools.partial(kernel, rows),
        out_shape=jax.ShapeDtypeStruct((frames, rows * cols, latent), jnp.bfloat16),
        in_specs=[vmem] * 5,
        out_specs=vmem,
        scratch_shapes=[
            pltpu.VMEM((count, wide * cols, channels), jnp.bfloat16),
            pltpu.VMEM((count, wide * cols, channels), jnp.bfloat16),
            pltpu.VMEM((count, (rows + 2) * cols, channels), jnp.bfloat16),
            pltpu.VMEM((count, (rows + 2) * cols, channels), jnp.bfloat16),
            pltpu.VMEM((3, 9 * BLK, BLK), jnp.bfloat16),
        ],
        compiler_params=pltpu.CompilerParams(vmem_limit_bytes=56 * 2**20),
    )(stack, weights, taps, norm_gain, head_weight)
    return output.reshape(1, frames, rows, merged)


def solution(mesh):
    return jax.shard_map(
        shards,
        mesh=mesh,
        in_specs=(
            P("span", None, "tile", None),
            P("span", None, "tile", None),
            P("span"),
            P("span", "tile", None),
            P("span", None),
            P(),
            P(),
            P(),
            P(),
            P(),
        ),
        out_specs=P("span", None, "tile", None),
        check_vma=False,
    )
```

time: 1030 us -> 105 us (0.10); the launches traced: 1020 us -> 104 us
  local copies, waits for them, and re-layouts: 552 us -> 21.5 us
  matrix products: 354 us -> 0.6 us
  loops' own time: 65.1 us -> 0 us
  Pallas kernels: 0 us -> 49 us
  other arithmetic: 18.4 us -> 5.49 us
    dot_general x75 -> x2, matrix products: 354 us -> 0.6 us  [select_frames(): jnp.einsum('sf,frm->srm', chosen.astype(jnp.bfloat16), frames, preferred_...]
    while x106 -> x0, local copies, waits for them, and re-layouts: 261 us -> none
    slice x83 -> x0, local copies, waits for them, and re-layouts: 197 us -> none  [the longest x72 130 us: one_frame(): plane[:, col_tap:col_tap + col_count]]
    another operation x2 -> x0, loops' own time: 65.1 us -> none  [causal_conv(): result = lax.map(one_frame, jnp.arange(frames, dtype=jnp.int32))]
    pallas_call x0 -> x1, Pallas kernels: none -> 49 us  [shards(): pl.pallas_call(functools.partial(kernel, rows), out_shape=jax.ShapeDtypeS...]
    another operation x4 -> x0, local copies, waits for them, and re-layouts: 18.8 us -> none  [the longest x2 10 us: causal_conv(): kernels = weight.reshape(3, 3, 3 * group_width, group_count, group_width)]
    pad x2 -> x0, local copies, waits for them, and re-layouts: 18.5 us -> none  [causal_conv(): padded = jnp.pad(active, ((2, 0), (0, 0), (1, 1), (0, 0)))]
    unnamed x23 -> x12, local copies, waits for them, and re-layouts: 19.6 us -> 1.59 us
  transfers between devices with their start and end apart: 7 -> 5, of which waited for: 1 -> 2; matrix products, arithmetic and copies ran while one was open for 3% -> 7% of each run, Pallas kernels for 0% -> 0%
where the time goes in v1:
time: 105 us; the launch traced here: 104 us
  Pallas kernels  49 us (47%)
  local copies, waits for them, and re-layouts  21.5 us (20%)
  starting transfers between devices  18.8 us (18%)
  waiting for transfers between devices  7.62 us (7%)
  other arithmetic  5.49 us (5%)
    pallas_call x1, Pallas kernels, shards(): pl.pallas_call(functools.partial(kernel, rows), out_shape=jax.ShapeDtypeS...  49 us
    reshape x1, local copies, waits for them, and re-layouts, shards(): stack.reshape(stack.shape[0], wide, cols, latent)  6.4 us
    transpose x1, local copies, waits for them, and re-layouts, shards(): jnp.transpose(stack.reshape(stack.shape[0], wide, cols, latent), (1, 2, 0...  5.92 us
    ppermute x1, starting transfers between devices, with_halo(): lax.ppermute(lax.slice_in_dim(block, block.shape[dim] - width, None, axis...  5.76 us
    all_to_all x1, starting transfers between devices, fetch_memory(): lax.all_to_all(request, 'span', split_axis=0, concat_axis=0, tiled=True)  4.27 us
    all_to_all x1, waiting for transfers between devices, fetch_memory(): lax.all_to_all(picked, 'span', split_axis=0, concat_axis=0, tiled=True)  4.16 us
    all_to_all x1, starting transfers between devices, fetch_memory(): lax.all_to_all(picked, 'span', split_axis=0, concat_axis=0, tiled=True)  3.45 us
    ppermute x1, waiting for transfers between devices, with_halo(): lax.ppermute(lax.slice_in_dim(block, 0, width, axis=dim), axis, backward)  3.45 us
  transfers between devices with their start and end apart: 5, of which 2 were waited for; matrix products, arithmetic and copies ran while one was open for 7% of the time, Pallas kernels for 0%

profile of v1, /device:TPU:1, one launch (start us, length us, event | category | flops | bytes accessed | tf_op | source)
XLA Modules:
  0.0 103.9 jit_solution(18093545269086249137)
XLA Ops:
  0.0 0.0 copy-start
  0.0 0.7 and_select_fusion.1
  0.7 0.7 and_select_fusion.2
  1.4 0.2 convert_reduce_fusion
  1.6 0.1 select_reduce_fusion
  1.7 0.7 sub.14
  2.4 4.3 %all-to-all-start = ((s32[4,1,4]{2,1,0:T(1,128)}), s32[4,1,4]{2,1,0:T(1,128)S(1)}, u32[]{:S(2)}, u32[]{:S(2)}) async-start(s32[4,1,4]{2,1,0:T(1,128)} %bitcast.6), calls=%async_computation | async-start | bytes 4096 | tf_op jit(solution)/shard_map/all_to_all | solution.py:61
  6.7 0.8 copy.56
  7.5 3.4 %collective-permute-start = (bf16[2,4,2560]{2,0,1:T(2,128)(2,1)S(1)}, bf16[2,4,2560]{2,0,1:T(2,128)(2,1)S(1)}, u32[]{:S(2)}, u32[]{:S(2)}) collective-permute-start(bf16[2,4,2560]{2,0,1:T(2,128)(2,1)S(1)} %bitcast.61), channel_id=1, source_target_pairs={{0,8},{8,16},{16,24},{1,9},{9,17},{17,25},{2,10},{10,18},{18,26},{... | collective-permute-start | bytes 122888 | tf_op jit(solution)/shard_map/ppermute | solution.py:19
  11.5 0.8 convert_multiply_fusion
  12.3 0.8 fusion.3
  13.2 0.0 all-to-all-done
  13.2 0.5 broadcast.145
  13.7 0.7 reduce.3
  14.3 0.1 eq.72
  14.4 0.0 copy-done
  14.4 0.3 convolution_convert_fusion.1
  14.7 0.1 reshape.95
  14.8 0.8 copy.35
  15.7 3.5 %all-to-all-start.1 = ((bf16[4,4,4,2560]{3,1,2,0:T(4,128)(2,1)}), bf16[4,4,4,2560]{3,1,2,0:T(4,128)(2,1)S(1)}, u32[]{:S(2)}, u32[]{:S(2)}) async-start(bf16[4,4,4,2560]{3,1,2,0:T(4,128)(2,1)} %copy.35), calls=%async_computation.1 | async-start | bytes 655360 | tf_op jit(solution)/shard_map/all_to_all | solution.py:65
  19.1 0.0 copy-start.2
  19.2 0.1 mul.58
  19.2 0.1 mul.59
  19.3 4.2 %all-to-all-done.1 = bf16[4,4,4,2560]{3,1,2,0:T(4,128)(2,1)S(1)} async-done(((bf16[4,4,4,2560]{3,1,2,0:T(4,128)(2,1)}), bf16[4,4,4,2560]{3,1,2,0:T(4,128)(2,1)S(1)}, u32[]{:S(2)}, u32[]{:S(2)}) %all-to-all-start.1) | async-done | bytes 327712 | tf_op jit(solution)/shard_map/all_to_all | solution.py:65
  23.5 0.1 copy.36
  23.6 0.0 copy-start.3
  23.6 0.0 copy-start.1
  23.6 0.1 reshape.96
  23.7 0.3 convolution_convert_fusion
  24.0 0.0 collective-permute-done
  24.0 0.1 pad_maximum_fusion.2
  24.2 5.8 %collective-permute-start.1 = (bf16[20,2,2560]{2,0,1:T(8,128)(2,1)S(1)}, bf16[20,2,2560]{2,0,1:T(8,128)(2,1)S(1)}, u32[]{:S(2)}, u32[]{:S(2)}) collective-permute-start(bf16[20,2,2560]{2,0,1:T(8,128)(2,1)S(1)} %get-tuple-element.5), channel_id=1, source_target_pairs={{0,1},{1,2},{2,3},{3,4},{4,5},{5,6},{6,7},{8,9},{9,10},{10,11},{11... | collective-permute-start | bytes 614408 | tf_op jit(solution)/shard_map/ppermute | solution.py:27
  29.9 1.9 %collective-permute-start.2 = (bf16[20,2,2560]{2,0,1:T(8,128)(2,1)S(1)}, bf16[20,2,2560]{2,0,1:T(8,128)(2,1)S(1)}, u32[]{:S(2)}, u32[]{:S(2)}) collective-permute-start(bf16[20,2,2560]{2,0,1:T(8,128)(2,1)S(1)} %get-tuple-element.6), channel_id=1, source_target_pairs={{1,0},{2,1},{3,2},{4,3},{5,4},{6,5},{7,6},{9,8},{10,9},{11,10},{12... | collective-permute-start | bytes 614408 | tf_op jit(solution)/shard_map/ppermute | solution.py:30
  31.9 0.1 broadcast_multiply_fusion
  32.0 0.8 copy.42.head_ref
  32.8 0.0 copy-done.1
  32.8 0.1 broadcast_in_dim.19
  32.9 1.1 %pad_maximum_fusion.w_ref = bf16[4,320,512]{2,1,0:T(8,128)(2,1)} fusion(bf16[4,64,512]{2,1,0:T(8,128)(2,1)S(1)} %broadcast_multiply_fusion, bf16[4,256,512]{2,1,0:T(8,128)(2,1)S(1)} %broadcast_in_dim.19), kind=kLoop, calls=%fused_computation.2 | loop fusion | flops 2621440 | bytes 2621440 | tf_op jit(solution)/shard_map/concatenate | solution.py:196
  34.0 0.0 collective-permute-done.1
  34.0 3.4 %collective-permute-done.2 = bf16[20,2,2560]{2,0,1:T(8,128)(2,1)S(1)} collective-permute-done((bf16[20,2,2560]{2,0,1:T(8,128)(2,1)S(1)}, bf16[20,2,2560]{2,0,1:T(8,128)(2,1)S(1)}, u32[]{:S(2)}, u32[]{:S(2)}) %collective-permute-start.2) | collective-permute-done | bytes 204832 | tf_op jit(solution)/shard_map/ppermute | solution.py:30
  37.5 0.1 pad_maximum_fusion.1
  37.6 0.2 copy.39
  37.8 6.4 %reshape.97 = bf16[20,8,160,16]{3,2,1,0:T(8,128)(2,1)} reshape(bf16[20,8,2560]{2,1,0:T(8,128)(2,1)S(1)} %copy.39) | data formatting | bytes 1638400 | tf_op jit(solution)/shard_map/reshape | solution.py:193
  44.2 5.9 %copy.40 = bf16[8,160,20,16]{1,0,3,2:T(8,128)(2,1)S(1)} copy(bf16[8,160,20,16]{3,1,0,2:T(8,128)(2,1)} %bitcast.57) | data formatting | bytes 1638400 | tf_op jit(solution)/shard_map/transpose | solution.py:192
  50.2 1.5 %reshape.98 = bf16[1280,320]{0,1:T(8,128)(2,1)S(1)} reshape(bf16[8,160,20,16]{1,0,3,2:T(8,128)(2,1)S(1)} %copy.40) | data formatting | bytes 1638400 | tf_op jit(solution)/shard_map/reshape | solution.py:194
  51.6 1.3 %copy.41.x_ref = bf16[1280,320]{1,0:T(8,128)(2,1)} copy(bf16[1280,320]{0,1:T(8,128)(2,1)S(1)} %reshape.98) | data formatting | bytes 1638400 | tf_op jit(solution)/shard_map/reshape | solution.py:194
  52.9 49.0 %shard_map.100 = bf16[2,640,16]{2,1,0:T(8,128)(2,1)} custom-call(bf16[1280,320]{1,0:T(8,128)(2,1)} %copy.41.x_ref, bf16[4,320,512]{2,1,0:T(8,128)(2,1)} %pad_maximum_fusion.w_ref, bf16[2,27,32,512]{3,2,1,0:T(8,128)(2,1)} %bitcast.58, f32[2,512]{1,0:T(2,128)} %gain_ref.1, bf16[512,16]{1,0:T(8,128)(2,1)} %copy.42.head_ref), custom_call_target="tpu_custom_call" | custom-call | tf_op jit(solution)/shard_map/pallas_call | solution.py:207
  101.9 1.9 %reshape.100 = bf16[1,2,4,2560]{3,2,1,0:T(4,128)(2,1)} reshape(bf16[2,640,16]{2,1,0:T(8,128)(2,1)} %shard_map.100) | data formatting | bytes 81920 | tf_op jit(solution)/shard_map/reshape | solution.py:221
  (10 shorter events, 0.1 us)
Async XLA Ops:
  0.0 14.4 %copy-start = (bf16[32,4,2560]{2,1,0:T(4,128)(2,1)S(1)}, bf16[32,4,2560]{2,1,0:T(4,128)(2,1)}, u32[]{:S(2)}) copy-start(bf16[32,4,2560]{2,1,0:T(4,128)(2,1)} %param.13) | copy-start | bytes 1966084
  0.0 19.3 %copy-start.4 = (s32[1,16]{1,0:T(1,128)S(1)}, s32[1,16]{1,0:T(1,128)}, u32[]{:S(2)}) copy-start(s32[1,16]{1,0:T(1,128)} %param.14) | copy-start | bytes 196
  2.4 10.8 %all-to-all-start = ((s32[4,1,4]{2,1,0:T(1,128)}), s32[4,1,4]{2,1,0:T(1,128)S(1)}, u32[]{:S(2)}, u32[]{:S(2)}) async-start(s32[4,1,4]{2,1,0:T(1,128)} %bitcast.6), calls=%async_computation | async-start | bytes 4096 | tf_op jit(solution)/shard_map/all_to_all | solution.py:61
  7.5 16.6 %collective-permute-start = (bf16[2,4,2560]{2,0,1:T(2,128)(2,1)S(1)}, bf16[2,4,2560]{2,0,1:T(2,128)(2,1)S(1)}, u32[]{:S(2)}, u32[]{:S(2)}) collective-permute-start(bf16[2,4,2560]{2,0,1:T(2,128)(2,1)S(1)} %bitcast.61), channel_id=1, source_target_pairs={{0,8},{8,16},{16,24},{1,9},{9,17},{17,25},{2,10},{10,18},{18,26},{... | collective-permute-start | bytes 122888 | tf_op jit(solution)/shard_map/ppermute | solution.py:19
  15.7 7.8 %all-to-all-start.1 = ((bf16[4,4,4,2560]{3,1,2,0:T(4,128)(2,1)}), bf16[4,4,4,2560]{3,1,2,0:T(4,128)(2,1)S(1)}, u32[]{:S(2)}, u32[]{:S(2)}) async-start(bf16[4,4,4,2560]{3,1,2,0:T(4,128)(2,1)} %copy.35), calls=%async_computation.1 | async-start | bytes 655360 | tf_op jit(solution)/shard_map/all_to_all | solution.py:65
  19.1 12.7 %copy-start.2 = (bf16[16,512]{1,0:T(8,128)(2,1)S(1)}, bf16[16,512]{1,0:T(8,128)(2,1)}, u32[]{:S(2)}) copy-start(bf16[16,512]{1,0:T(8,128)(2,1)} %param.15) | copy-start | bytes 49156
  23.6 8.4 %copy-start.3 = (bf16[512,16]{0,1:T(8,128)(2,1)S(1)}, bf16[512,16]{0,1:T(8,128)(2,1)}, u32[]{:S(2)}) copy-start(bf16[512,16]{0,1:T(8,128)(2,1)} %param.19) | copy-start | bytes 49156
  23.6 9.1 %copy-start.1 = (bf16[256,512]{1,0:T(8,128)(2,1)S(1)}, bf16[256,512]{1,0:T(8,128)(2,1)}, u32[]{:S(2)}) copy-start(bf16[256,512]{1,0:T(8,128)(2,1)} %param.16) | copy-start | bytes 786436
  24.2 9.8 %collective-permute-start.1 = (bf16[20,2,2560]{2,0,1:T(8,128)(2,1)S(1)}, bf16[20,2,2560]{2,0,1:T(8,128)(2,1)S(1)}, u32[]{:S(2)}, u32[]{:S(2)}) collective-permute-start(bf16[20,2,2560]{2,0,1:T(8,128)(2,1)S(1)} %get-tuple-element.5), channel_id=1, source_target_pairs={{0,1},{1,2},{2,3},{3,4},{4,5},{5,6},{6,7},{8,9},{9,10},{10,11},{11... | collective-permute-start | bytes 614408 | tf_op jit(solution)/shard_map/ppermute | solution.py:27
  29.9 7.5 %collective-permute-start.2 = (bf16[20,2,2560]{2,0,1:T(8,128)(2,1)S(1)}, bf16[20,2,2560]{2,0,1:T(8,128)(2,1)S(1)}, u32[]{:S(2)}, u32[]{:S(2)}) collective-permute-start(bf16[20,2,2560]{2,0,1:T(8,128)(2,1)S(1)} %get-tuple-element.6), channel_id=1, source_target_pairs={{1,0},{2,1},{3,2},{4,3},{5,4},{6,5},{7,6},{9,8},{10,9},{11,10},{12... | collective-permute-start | bytes 614408 | tf_op jit(solution)/shard_map/ppermute | solution.py:30

commit v2 on v1

--- a/solution.py
+++ b/solution.py
@@ -10,7 +10,8 @@
 CTX = 2
 CAP = 4
 BLK = 256
-CHUNK = 2
+CHUNK1 = 6
+CHUNK2 = 4
 
 
 def shifted(value, axis, steps):
@@ -66,9 +67,14 @@
     return select_frames(returned.reshape(span_count * CAP, row_count, merged), reply_slot)
 
 
-def kernel(rows, x_ref, w_ref, cw_ref, gain_ref, head_ref, out_ref, h0, a1, h1, a2, wexp):
+def kernel(
+    rows, x_ref, stem_ref, mem_ref, cw_ref, gain_ref, head_ref, out_ref, hf, wt, h0, a1, h1, a2, wexp
+):
     frames = h0.shape[0]
-    cols = x_ref.shape[0] // (rows + 4)
+    latent = stem_ref.shape[0]
+    spread = 128 // latent
+    mems = x_ref.shape[0] - frames
+    cols = x_ref.shape[1] // (rows + 4) * spread
     tile = lax.axis_index("tile")
     total_rows = lax.axis_size("tile") * rows
 
@@ -78,13 +84,31 @@
         half = values * scale * (0.5 * gain_ref[layer : layer + 1, :])
         return half * (1.0 + jnp.tanh(half))
 
+    for member in range(mems):
+        narrow = mem_ref[member * latent : (member + 1) * latent, :]
+        wt[member * 128 : (member + 1) * 128, :] = jnp.concatenate([narrow] * spread, axis=0)
+    stem = jnp.concatenate([stem_ref[...]] * spread, axis=0)
+    chunks = x_ref.shape[1]
+    lane_column = lax.broadcasted_iota(jnp.int32, (16, 128), 1) // latent
+    for place in range(spread):
+        mask = (lane_column == place).astype(jnp.float32).astype(jnp.bfloat16)[:1]
+        stacked = jnp.concatenate([x_ref[member] * mask for member in range(mems)], axis=1)
+        memory_term = jnp.dot(stacked, wt[...], preferred_element_type=jnp.float32)
+        for frame in range(frames):
+            term = memory_term + jnp.dot(
+                x_ref[mems + frame] * mask, stem, preferred_element_type=jnp.float32
+            )
+            for lane in range(term.shape[1] // 128):
+                hf[frame, lane, pl.ds(place, chunks, stride=spread), :] = term[
+                    :, lane * 128 : (lane + 1) * 128
+                ]
+
     @pl.loop(0, rows + 4)
     def _(row):
         at = pl.ds(pl.multiple_of(row * cols, 16), cols)
-        stacked = x_ref[at, :]
         for frame in range(frames):
-            hidden = jnp.dot(
-                stacked, w_ref[frame], preferred_element_type=jnp.float32
+            hidden = jnp.concatenate(
+                [hf[frame, lane, at, :] for lane in range(hf.shape[1])], axis=1
             ).astype(jnp.bfloat16)
             h0[frame, at, :] = hidden
             a1[frame, at, :] = activate(hidden, 0).astype(jnp.bfloat16)
@@ -92,10 +116,10 @@
     in_group = lax.broadcasted_iota(jnp.int32, (BLK, BLK), 0) // 32
     out_group = lax.broadcasted_iota(jnp.int32, (BLK, BLK), 1) // 32
     diagonal = (in_group == out_group).astype(jnp.float32).astype(jnp.bfloat16)
-    size = CHUNK * cols
-    column = lax.rem(lax.broadcasted_iota(jnp.int32, (size, BLK), 0), cols)
-
-    def conv(layer, source, base, first_frame, row_count, target):
+    def conv(layer, source, base, first_frame, row_count, target, chunk_rows):
+        size = chunk_rows * cols
+        column = lax.rem(lax.broadcasted_iota(jnp.int32, (size, BLK), 0), cols)
+
         @pl.loop(0, 2)
         def _(half):
             lanes = pl.ds(pl.multiple_of(half * BLK, BLK), BLK)
@@ -108,7 +132,7 @@
                     wexp[dx, pl.ds(pl.multiple_of(tap * BLK, BLK), BLK), :] = wide * diagonal
 
             def one_frame(frame, taps):
-                @pl.loop(0, row_count // CHUNK)
+                @pl.loop(0, row_count // chunk_rows)
                 def _(chunk):
                     start = chunk * size
                     pieces = [
@@ -145,7 +169,7 @@
                 one_frame(frame, frame + 1)
             pl.loop(2, frames)(lambda frame: one_frame(frame, 3))
 
-    conv(0, a1, h0, 0, rows + 2, h1)
+    conv(0, a1, h0, 0, rows + 2, h1, CHUNK1 if (rows + 2) % CHUNK1 == 0 else 1)
 
     @pl.loop(0, rows + 2)
     def _(row):
@@ -155,7 +179,7 @@
         for frame in range(frames):
             a2[frame, at, :] = (activate(h1[frame, at, :], 1) * keep).astype(jnp.bfloat16)
 
-    conv(1, a2, h1, CTX, rows, h0)
+    conv(1, a2, h1, CTX, rows, h0, CHUNK2 if rows % CHUNK2 == 0 else 1)
 
     for frame in range(frames - CTX):
         out_ref[frame] = jnp.dot(
@@ -187,29 +211,19 @@
     memory = fetch_memory(memory_bank, memory_index)
     stack = jnp.concatenate([memory, previous, noisy], axis=0)
     stack = with_halo(stack, (("tile", 1),), 2)
-    depth = stack.shape[0] * latent
     wide = rows + 4
-    stack = jnp.transpose(
-        stack.reshape(stack.shape[0], wide, cols, latent), (1, 2, 0, 3)
-    ).reshape(wide * cols, depth)
     count = CTX + frames
-    weights = jnp.concatenate(
-        [
-            jnp.broadcast_to(memory_weight[None], (count,) + memory_weight.shape),
-            (
-                jnp.eye(count, dtype=jnp.bfloat16)[:, :, None, None] * stem_weight[None, None]
-            ).reshape(count, count * latent, channels),
-        ],
-        axis=1,
-    )
+    stack = stack.reshape(stack.shape[0], wide * merged // 128, 128)
     taps = conv_weight.reshape(conv_weight.shape[0], 27, conv_weight.shape[4], channels)
     vmem = pl.BlockSpec(memory_space=pltpu.VMEM)
     output = pl.pallas_call(
         functools.partial(kernel, rows),
         out_shape=jax.ShapeDtypeStruct((frames, rows * cols, latent), jnp.bfloat16),
-        in_specs=[vmem] * 5,
+        in_specs=[vmem] * 6,
         out_specs=vmem,
         scratch_shapes=[
+            pltpu.VMEM((count, channels // 128, wide * cols, 128), jnp.float32),
+            pltpu.VMEM((memory.shape[0] * 128, channels), jnp.bfloat16),
             pltpu.VMEM((count, wide * cols, channels), jnp.bfloat16),
             pltpu.VMEM((count, wide * cols, channels), jnp.bfloat16),
             pltpu.VMEM((count, (rows + 2) * cols, channels), jnp.bfloat16),
@@ -217,7 +231,7 @@
             pltpu.VMEM((3, 9 * BLK, BLK), jnp.bfloat16),
         ],
         compiler_params=pltpu.CompilerParams(vmem_limit_bytes=56 * 2**20),
-    )(stack, weights, taps, norm_gain, head_weight)
+    )(stack, stem_weight, memory_weight, taps, norm_gain, head_weight)
     return output.reshape(1, frames, rows, merged)
 
 

time: 105 us -> 89.8 us (0.86)
  local copies, waits for them, and re-layouts: 21.5 us -> 8.06 us
  other arithmetic: 5.49 us -> 3.45 us
  waiting for transfers between devices: 7.62 us -> 9.07 us
    reshape x3 -> x1, local copies, waits for them, and re-layouts: 9.16 us -> 1.88 us  [shards(): stack = stack.reshape(stack.shape[0], wide * merged // 128, 128)]
    transpose x1 -> x0, local copies, waits for them, and re-layouts: 5.92 us -> none  [shards(): jnp.transpose(stack.reshape(stack.shape[0], wide, cols, latent), (1, 2, 0...]
    concatenate x1 -> x0, other arithmetic: 1.15 us -> none  [shards(): jnp.concatenate([jnp.broadcast_to(memory_weight[None], (count,) + memory_...]
  transfers between devices with their start and end apart: 5 -> 5, of which waited for: 2 -> 3; matrix products, arithmetic and copies ran while one was open for 7% -> 6% of each run, Pallas kernels for 0% -> 0%
where the time goes in v2:
time: 89.8 us; the launch traced here: 89.3 us
  Pallas kernels  48.5 us (54%)
  starting transfers between devices  18.8 us (21%)
  waiting for transfers between devices  9.07 us (10%)
  local copies, waits for them, and re-layouts  8.06 us (9%)
  other arithmetic  3.45 us (4%)
    pallas_call x1, Pallas kernels, shards(): pl.pallas_call(functools.partial(kernel, rows), out_shape=jax.ShapeDtypeS...  48.5 us
    ppermute x1, starting transfers between devices, with_halo(): lax.ppermute(lax.slice_in_dim(block, block.shape[dim] - width, None, axis...  5.75 us
    ppermute x1, waiting for transfers between devices, with_halo(): lax.ppermute(lax.slice_in_dim(block, 0, width, axis=dim), axis, backward)  4.4 us
    all_to_all x1, starting transfers between devices, fetch_memory(): lax.all_to_all(request, 'span', split_axis=0, concat_axis=0, tiled=True)  4.27 us
    all_to_all x1, waiting for transfers between devices, fetch_memory(): lax.all_to_all(picked, 'span', split_axis=0, concat_axis=0, tiled=True)  4.25 us
    all_to_all x1, starting transfers between devices, fetch_memory(): lax.all_to_all(picked, 'span', split_axis=0, concat_axis=0, tiled=True)  3.45 us
    ppermute x1, starting transfers between devices, shifted(): lax.ppermute(value, axis, [(source, source + steps) for source in range(f...  3.37 us
    reshape x1, local copies, waits for them, and re-layouts, shards(): return output.reshape(1, frames, rows, merged)  1.94 us
  transfers between devices with their start and end apart: 5, of which 3 were waited for; matrix products, arithmetic and copies ran while one was open for 6% of the time, Pallas kernels for 0%

profile of v2, /device:TPU:1, one launch (start us, length us, event | category | flops | bytes accessed | tf_op | source)
XLA Modules:
  0.0 89.3 jit_solution(8204671324847907916)
XLA Ops:
  0.0 0.0 copy-start
  0.0 0.0 copy-start.3
  0.0 0.0 copy-start.1
  0.0 0.7 and_select_fusion.1
  0.8 0.7 and_select_fusion.2
  1.4 0.2 convert_reduce_fusion
  1.6 0.1 select_reduce_fusion
  1.7 0.7 sub.14
  2.4 4.3 %all-to-all-start = ((s32[4,1,4]{2,1,0:T(1,128)}), s32[4,1,4]{2,1,0:T(1,128)S(1)}, u32[]{:S(2)}, u32[]{:S(2)}) async-start(s32[4,1,4]{2,1,0:T(1,128)} %bitcast.6), calls=%async_computation | async-start | bytes 4096 | tf_op jit(solution)/shard_map/all_to_all | solution.py:62
  6.7 0.8 copy.50
  7.5 3.4 %collective-permute-start = (bf16[2,4,2560]{2,0,1:T(2,128)(2,1)S(1)}, bf16[2,4,2560]{2,0,1:T(2,128)(2,1)S(1)}, u32[]{:S(2)}, u32[]{:S(2)}) collective-permute-start(bf16[2,4,2560]{2,0,1:T(2,128)(2,1)S(1)} %bitcast.53), channel_id=1, source_target_pairs={{0,8},{8,16},{16,24},{1,9},{9,17},{17,25},{2,10},{10,18},{18,26},{... | collective-permute-start | bytes 122888 | tf_op jit(solution)/shard_map/ppermute | solution.py:20
  11.5 0.8 convert_multiply_fusion
  12.3 0.0 all-to-all-done
  12.3 0.5 broadcast.139
  12.9 0.7 reduce.3
  13.5 0.1 eq.65
  13.6 0.0 copy-done
  13.6 0.3 convolution_convert_fusion.1
  13.9 0.1 reshape.79
  14.0 0.8 copy.31
  14.8 3.5 %all-to-all-start.1 = ((bf16[4,4,4,2560]{3,1,2,0:T(4,128)(2,1)}), bf16[4,4,4,2560]{3,1,2,0:T(4,128)(2,1)S(1)}, u32[]{:S(2)}, u32[]{:S(2)}) async-start(bf16[4,4,4,2560]{3,1,2,0:T(4,128)(2,1)} %copy.31), calls=%async_computation.1 | async-start | bytes 655360 | tf_op jit(solution)/shard_map/all_to_all | solution.py:66
  18.3 0.0 copy-done.1
  18.3 0.1 fusion.3
  18.4 0.0 copy-done.3
  18.4 0.0 copy-start.2
  18.4 4.3 %all-to-all-done.1 = bf16[4,4,4,2560]{3,1,2,0:T(4,128)(2,1)S(1)} async-done(((bf16[4,4,4,2560]{3,1,2,0:T(4,128)(2,1)}), bf16[4,4,4,2560]{3,1,2,0:T(4,128)(2,1)S(1)}, u32[]{:S(2)}, u32[]{:S(2)}) %all-to-all-start.1) | async-done | bytes 327712 | tf_op jit(solution)/shard_map/all_to_all | solution.py:66
  22.7 0.1 copy.32
  22.8 0.1 reshape.80
  22.9 0.3 convolution_convert_fusion
  23.2 0.0 collective-permute-done
  23.2 0.1 pad_maximum_fusion.1
  23.3 5.8 %collective-permute-start.1 = (bf16[20,2,2560]{2,0,1:T(8,128)(2,1)S(1)}, bf16[20,2,2560]{2,0,1:T(8,128)(2,1)S(1)}, u32[]{:S(2)}, u32[]{:S(2)}) collective-permute-start(bf16[20,2,2560]{2,0,1:T(8,128)(2,1)S(1)} %get-tuple-element.5), channel_id=1, source_target_pairs={{0,1},{1,2},{2,3},{3,4},{4,5},{5,6},{6,7},{8,9},{9,10},{10,11},{11... | collective-permute-start | bytes 614408 | tf_op jit(solution)/shard_map/ppermute | solution.py:28
  29.1 1.9 %collective-permute-start.2 = (bf16[20,2,2560]{2,0,1:T(8,128)(2,1)S(1)}, bf16[20,2,2560]{2,0,1:T(8,128)(2,1)S(1)}, u32[]{:S(2)}, u32[]{:S(2)}) collective-permute-start(bf16[20,2,2560]{2,0,1:T(8,128)(2,1)S(1)} %get-tuple-element.6), channel_id=1, source_target_pairs={{1,0},{2,1},{3,2},{4,3},{5,4},{6,5},{7,6},{9,8},{10,9},{11,10},{12... | collective-permute-start | bytes 614408 | tf_op jit(solution)/shard_map/ppermute | solution.py:31
  31.0 0.0 copy-done.2
  31.0 0.8 copy.36.head_ref
  31.8 0.4 collective-permute-done.1
  32.2 4.4 %collective-permute-done.2 = bf16[20,2,2560]{2,0,1:T(8,128)(2,1)S(1)} collective-permute-done((bf16[20,2,2560]{2,0,1:T(8,128)(2,1)S(1)}, bf16[20,2,2560]{2,0,1:T(8,128)(2,1)S(1)}, u32[]{:S(2)}, u32[]{:S(2)}) %collective-permute-start.2) | collective-permute-done | bytes 204832 | tf_op jit(solution)/shard_map/ppermute | solution.py:31
  36.6 0.1 pad_maximum_fusion
  36.7 0.2 copy.35
  37.0 1.9 %reshape.81.x_ref = bf16[20,160,128]{2,1,0:T(8,128)(2,1)} reshape(bf16[20,8,2560]{2,1,0:T(8,128)(2,1)S(1)} %copy.35) | data formatting | bytes 1638400 | tf_op jit(solution)/shard_map/reshape | solution.py:216
  38.8 48.5 %shard_map.100 = bf16[2,640,16]{2,1,0:T(8,128)(2,1)} custom-call(bf16[20,160,128]{2,1,0:T(8,128)(2,1)} %reshape.81.x_ref, bf16[16,512]{1,0:T(8,128)(2,1)} %stem_ref.1, bf16[256,512]{1,0:T(8,128)(2,1)} %mem_ref.1, bf16[2,27,32,512]{3,2,1,0:T(8,128)(2,1)} %bitcast.51, f32[2,512]{1,0:T(2,128)} %gain_ref.1, bf16[512,16]{1,0:T(8,128)(2,1)} %copy.36.head_ref), custom_call_target="tpu_custom_call" | custom-call | tf_op jit(solution)/shard_map/pallas_call | solution.py:219
  87.3 1.9 %reshape.83 = bf16[1,2,4,2560]{3,2,1,0:T(4,128)(2,1)} reshape(bf16[2,640,16]{2,1,0:T(8,128)(2,1)} %shard_map.100) | data formatting | bytes 81920 | tf_op jit(solution)/shard_map/reshape | solution.py:235
  (4 shorter events, 0.1 us)
Async XLA Ops:
  0.0 13.6 %copy-start = (bf16[32,4,2560]{2,1,0:T(4,128)(2,1)S(1)}, bf16[32,4,2560]{2,1,0:T(4,128)(2,1)}, u32[]{:S(2)}) copy-start(bf16[32,4,2560]{2,1,0:T(4,128)(2,1)} %param.13) | copy-start | bytes 1966084
  0.0 18.4 %copy-start.3 = (s32[1,16]{1,0:T(1,128)S(1)}, s32[1,16]{1,0:T(1,128)}, u32[]{:S(2)}) copy-start(s32[1,16]{1,0:T(1,128)} %param.14) | copy-start | bytes 196
  0.0 18.3 %copy-start.1 = (bf16[1,2,4,2560]{3,2,1,0:T(4,128)(2,1)S(1)}, bf16[1,2,4,2560]{3,2,1,0:T(4,128)(2,1)}, u32[]{:S(2)}) copy-start(bf16[1,2,4,2560]{3,2,1,0:T(4,128)(2,1)} %param.10) | copy-start | bytes 122884
  2.4 9.9 %all-to-all-start = ((s32[4,1,4]{2,1,0:T(1,128)}), s32[4,1,4]{2,1,0:T(1,128)S(1)}, u32[]{:S(2)}, u32[]{:S(2)}) async-start(s32[4,1,4]{2,1,0:T(1,128)} %bitcast.6), calls=%async_computation | async-start | bytes 4096 | tf_op jit(solution)/shard_map/all_to_all | solution.py:62
  7.5 15.7 %collective-permute-start = (bf16[2,4,2560]{2,0,1:T(2,128)(2,1)S(1)}, bf16[2,4,2560]{2,0,1:T(2,128)(2,1)S(1)}, u32[]{:S(2)}, u32[]{:S(2)}) collective-permute-start(bf16[2,4,2560]{2,0,1:T(2,128)(2,1)S(1)} %bitcast.53), channel_id=1, source_target_pairs={{0,8},{8,16},{16,24},{1,9},{9,17},{17,25},{2,10},{10,18},{18,26},{... | collective-permute-start | bytes 122888 | tf_op jit(solution)/shard_map/ppermute | solution.py:20
  14.8 7.8 %all-to-all-start.1 = ((bf16[4,4,4,2560]{3,1,2,0:T(4,128)(2,1)}), bf16[4,4,4,2560]{3,1,2,0:T(4,128)(2,1)S(1)}, u32[]{:S(2)}, u32[]{:S(2)}) async-start(bf16[4,4,4,2560]{3,1,2,0:T(4,128)(2,1)} %copy.31), calls=%async_computation.1 | async-start | bytes 655360 | tf_op jit(solution)/shard_map/all_to_all | solution.py:66
  18.4 12.6 %copy-start.2 = (bf16[512,16]{0,1:T(8,128)(2,1)S(1)}, bf16[512,16]{0,1:T(8,128)(2,1)}, u32[]{:S(2)}) copy-start(bf16[512,16]{0,1:T(8,128)(2,1)} %param.19) | copy-start | bytes 49156
  23.3 8.9 %collective-permute-start.1 = (bf16[20,2,2560]{2,0,1:T(8,128)(2,1)S(1)}, bf16[20,2,2560]{2,0,1:T(8,128)(2,1)S(1)}, u32[]{:S(2)}, u32[]{:S(2)}) collective-permute-start(bf16[20,2,2560]{2,0,1:T(8,128)(2,1)S(1)} %get-tuple-element.5), channel_id=1, source_target_pairs={{0,1},{1,2},{2,3},{3,4},{4,5},{5,6},{6,7},{8,9},{9,10},{10,11},{11... | collective-permute-start | bytes 614408 | tf_op jit(solution)/shard_map/ppermute | solution.py:28
  29.1 7.5 %collective-permute-start.2 = (bf16[20,2,2560]{2,0,1:T(8,128)(2,1)S(1)}, bf16[20,2,2560]{2,0,1:T(8,128)(2,1)S(1)}, u32[]{:S(2)}, u32[]{:S(2)}) collective-permute-start(bf16[20,2,2560]{2,0,1:T(8,128)(2,1)S(1)} %get-tuple-element.6), channel_id=1, source_target_pairs={{1,0},{2,1},{3,2},{4,3},{5,4},{6,5},{7,6},{9,8},{10,9},{11,10},{12... | collective-permute-start | bytes 614408 | tf_op jit(solution)/shard_map/ppermute | solution.py:31

commit v3 on v2

--- a/solution.py
+++ b/solution.py
@@ -132,13 +132,12 @@
                     wexp[dx, pl.ds(pl.multiple_of(tap * BLK, BLK), BLK), :] = wide * diagonal
 
             def one_frame(frame, taps):
-                @pl.loop(0, row_count // chunk_rows)
-                def _(chunk):
+                def one_chunk(chunk):
                     start = chunk * size
                     pieces = [
                         source[
                             frame + dt - 2,
-                            pl.ds(pl.multiple_of(start + dy * cols, 16), size),
+                            pl.ds(start + dy * cols, size),
                             lanes,
                         ]
                         for dt in range(3 - taps, 3)
@@ -146,7 +145,7 @@
                     ]
                     joined = jnp.concatenate(pieces, axis=1)
                     total = base[
-                        frame, pl.ds(pl.multiple_of(start + cols, 16), size), lanes
+                        frame, pl.ds(start + cols, size), lanes
                     ].astype(jnp.float32)
                     for dx in range(3):
                         term = jnp.dot(
@@ -162,12 +161,14 @@
                             )
                         total = total + term
                     target[
-                        frame - first_frame, pl.ds(pl.multiple_of(start, 16), size), lanes
+                        frame - first_frame, pl.ds(start, size), lanes
                     ] = total.astype(jnp.bfloat16)
 
-            for frame in range(first_frame, min(2, frames)):
-                one_frame(frame, frame + 1)
-            pl.loop(2, frames)(lambda frame: one_frame(frame, 3))
+                for chunk in range(row_count // chunk_rows):
+                    one_chunk(chunk)
+
+            for frame in range(first_frame, frames):
+                one_frame(frame, min(frame + 1, 3))
 
     conv(0, a1, h0, 0, rows + 2, h1, CHUNK1 if (rows + 2) % CHUNK1 == 0 else 1)
 
@@ -208,9 +209,9 @@
         * lax.rsqrt(1.0 + sigma * sigma)
     ).astype(jnp.bfloat16)
     previous = shifted(clean_latents[0, frames - CTX :], "span", 1)
-    memory = fetch_memory(memory_bank, memory_index)
-    stack = jnp.concatenate([memory, previous, noisy], axis=0)
-    stack = with_halo(stack, (("tile", 1),), 2)
+    memory = fetch_memory(with_halo(memory_bank, (("tile", 1),), 2), memory_index)
+    sequence = with_halo(jnp.concatenate([previous, noisy], axis=0), (("tile", 1),), 2)
+    stack = jnp.concatenate([memory, sequence], axis=0)
     wide = rows + 4
     count = CTX + frames
     stack = stack.reshape(stack.shape[0], wide * merged // 128, 128)

time: 89.8 us -> 88 us (0.980); the launches traced: 89.3 us -> 86.5 us
  waiting for transfers between devices: 9.07 us -> 3.32 us
  starting transfers between devices: 18.8 us -> 22.5 us
  Pallas kernels: 48.5 us -> 47.4 us
    all_to_all x1, waiting for transfers between devices: 4.25 us -> 1.29 us  [fetch_memory(): lax.all_to_all(picked, 'span', split_axis=0, concat_axis=0, tiled=True)]
    ppermute x1 -> x2, waiting for transfers between devices: 4.4 us -> 2.03 us  [with_halo(): lax.ppermute(lax.slice_in_dim(block, 0, width, axis=dim), axis, backward)]
    ppermute x1 -> x2, starting transfers between devices: 1.92 us -> 3.84 us  [with_halo(): lax.ppermute(lax.slice_in_dim(block, 0, width, axis=dim), axis, backward)]
    ppermute x1 -> x2, starting transfers between devices: 5.75 us -> 6.86 us  [with_halo(): lax.ppermute(lax.slice_in_dim(block, block.shape[dim] - width, None, axis...]
    pallas_call x1, Pallas kernels: 48.5 us -> 47.4 us  [shards(): pl.pallas_call(functools.partial(kernel, rows), out_shape=jax.ShapeDtypeS...]
    unnamed x10 -> x11, local copies, waits for them, and re-layouts: 1.59 us -> 2 us
  transfers between devices with their start and end apart: 5 -> 7, of which waited for: 3 -> 3; matrix products, arithmetic and copies ran while one was open for 6% -> 7% of each run, Pallas kernels for 0% -> 0%
where the time goes in v3:
time: 88 us; the launch traced here: 86.5 us
  Pallas kernels  47.4 us (54%)
  starting transfers between devices  22.5 us (26%)
  local copies, waits for them, and re-layouts  8.95 us (10%)
  waiting for transfers between devices  3.32 us (4%)
  other arithmetic  2.6 us (3%)
    pallas_call x1, Pallas kernels, shards(): pl.pallas_call(functools.partial(kernel, rows), out_shape=jax.ShapeDtypeS...  47.4 us
    ppermute x2, starting transfers between devices, with_halo(): lax.ppermute(lax.slice_in_dim(block, block.shape[dim] - width, None, axis...  6.86 us
    all_to_all x1, starting transfers between devices, fetch_memory(): lax.all_to_all(request, 'span', split_axis=0, concat_axis=0, tiled=True)  4.27 us
    all_to_all x1, starting transfers between devices, fetch_memory(): lax.all_to_all(picked, 'span', split_axis=0, concat_axis=0, tiled=True)  3.91 us
    ppermute x2, starting transfers between devices, with_halo(): lax.ppermute(lax.slice_in_dim(block, 0, width, axis=dim), axis, backward)  3.84 us
    ppermute x1, starting transfers between devices, shifted(): lax.ppermute(value, axis, [(source, source + steps) for source in range(f...  3.65 us
    ppermute x2, waiting for transfers between devices, with_halo(): lax.ppermute(lax.slice_in_dim(block, 0, width, axis=dim), axis, backward)  2.03 us
    unnamed x11, local copies, waits for them, and re-layouts  2 us
  transfers between devices with their start and end apart: 7, of which 3 were waited for; matrix products, arithmetic and copies ran while one was open for 7% of the time, Pallas kernels for 0%

profile of v3, /device:TPU:1, one launch (start us, length us, event | category | flops | bytes accessed | tf_op | source)
XLA Modules:
  0.0 86.5 jit_solution(12477546092594896325)
XLA Ops:
  0.0 0.0 copy-start
  0.0 0.0 copy-start.1
  0.0 0.7 and_select_fusion.1
  0.7 0.7 and_select_fusion.2
  1.3 0.2 convert_reduce_fusion
  1.5 0.1 select_reduce_fusion
  1.7 0.7 sub.14
  2.3 4.3 %all-to-all-start = ((s32[4,1,4]{2,1,0:T(1,128)}), s32[4,1,4]{2,1,0:T(1,128)S(1)}, u32[]{:S(2)}, u32[]{:S(2)}) async-start(s32[4,1,4]{2,1,0:T(1,128)} %bitcast.6), calls=%async_computation | async-start | bytes 4096 | tf_op jit(solution)/shard_map/all_to_all | solution.py:62
  6.6 1.2 %copy.36 = bf16[32,4,2560]{2,0,1:T(8,128)(2,1)S(1)} copy(bf16[32,4,2560]{2,1,0:T(4,128)(2,1)} %param.13) | data formatting | bytes 1310720 | tf_op args[3]
  7.8 4.0 %collective-permute-start = (bf16[32,2,2560]{2,0,1:T(8,128)(2,1)S(1)}, bf16[32,2,2560]{2,0,1:T(8,128)(2,1)S(1)}, u32[]{:S(2)}, u32[]{:S(2)}) collective-permute-start(bf16[32,2,2560]{2,0,1:T(8,128)(2,1)S(1)} %get-tuple-element.5), channel_id=1, source_target_pairs={{0,1},{1,2},{2,3},{3,4},{4,5},{5,6},{6,7},{8,9},{9,10},{10,11},{11... | collective-permute-start | bytes 983048 | tf_op jit(solution)/shard_map/ppermute | solution.py:28
  11.9 1.9 %collective-permute-start.1 = (bf16[32,2,2560]{2,0,1:T(8,128)(2,1)S(1)}, bf16[32,2,2560]{2,0,1:T(8,128)(2,1)S(1)}, u32[]{:S(2)}, u32[]{:S(2)}) collective-permute-start(bf16[32,2,2560]{2,0,1:T(8,128)(2,1)S(1)} %get-tuple-element.6), channel_id=1, source_target_pairs={{1,0},{2,1},{3,2},{4,3},{5,4},{6,5},{7,6},{9,8},{10,9},{11,10},{12... | collective-permute-start | bytes 983048 | tf_op jit(solution)/shard_map/ppermute | solution.py:31
  13.8 0.0 copy-done
  13.9 3.6 %collective-permute-start.2 = (bf16[2,4,2560]{2,0,1:T(2,128)(2,1)S(1)}, bf16[2,4,2560]{2,0,1:T(2,128)(2,1)S(1)}, u32[]{:S(2)}, u32[]{:S(2)}) collective-permute-start(bf16[2,4,2560]{2,0,1:T(2,128)(2,1)S(1)} %bitcast.53), channel_id=1, source_target_pairs={{0,8},{8,16},{16,24},{1,9},{9,17},{17,25},{2,10},{10,18},{18,26},{... | collective-permute-start | bytes 122888 | tf_op jit(solution)/shard_map/ppermute | solution.py:20
  18.2 0.0 copy-done.1
  18.2 0.1 fusion.7
  18.3 0.0 all-to-all-done
  18.3 0.5 broadcast.139
  18.8 0.7 reduce.3
  19.5 0.1 eq.65
  19.6 0.0 collective-permute-done
  19.6 0.7 collective-permute-done.1
  20.3 0.4 convolution_convert_fusion.1
  20.7 0.0 copy-start.3
  20.7 0.0 copy-start.2
  20.7 0.2 reshape.79
  20.9 1.1 %copy.39 = bf16[4,4,8,2560]{3,1,2,0:T(4,128)(2,1)} copy(bf16[4,4,8,2560]{3,1,0,2:T(4,128)(2,1)S(1)} %reshape.79) | data formatting | bytes 1310720 | tf_op jit(solution)/shard_map/reshape | solution.py:63
  21.9 3.9 %all-to-all-start.1 = ((bf16[4,4,8,2560]{3,1,2,0:T(4,128)(2,1)}), bf16[4,4,8,2560]{3,1,2,0:T(4,128)(2,1)S(1)}, u32[]{:S(2)}, u32[]{:S(2)}) async-start(bf16[4,4,8,2560]{3,1,2,0:T(4,128)(2,1)} %copy.39), calls=%async_computation.1 | async-start | bytes 1310720 | tf_op jit(solution)/shard_map/all_to_all | solution.py:66
  25.8 0.0 copy-done.3
  25.8 0.0 copy-done.2
  25.9 0.8 copy.44.head_ref
  26.6 0.0 collective-permute-done.2
  26.6 0.1 fusion.8
  26.7 2.8 %collective-permute-start.3 = (bf16[4,2,2560]{2,0,1:T(4,128)(2,1)S(1)}, bf16[4,2,2560]{2,0,1:T(4,128)(2,1)S(1)}, u32[]{:S(2)}, u32[]{:S(2)}) collective-permute-start(bf16[4,2,2560]{2,0,1:T(4,128)(2,1)S(1)} %get-tuple-element.7), channel_id=1, source_target_pairs={{0,1},{1,2},{2,3},{3,4},{4,5},{5,6},{6,7},{8,9},{9,10},{10,11},{11... | collective-permute-start | bytes 122888 | tf_op jit(solution)/shard_map/ppermute | solution.py:28
  29.5 1.9 %collective-permute-start.4 = (bf16[4,2,2560]{2,0,1:T(4,128)(2,1)S(1)}, bf16[4,2,2560]{2,0,1:T(4,128)(2,1)S(1)}, u32[]{:S(2)}, u32[]{:S(2)}) collective-permute-start(bf16[4,2,2560]{2,0,1:T(4,128)(2,1)S(1)} %get-tuple-element.8), channel_id=1, source_target_pairs={{1,0},{2,1},{3,2},{4,3},{5,4},{6,5},{7,6},{9,8},{10,9},{11,10},{12... | collective-permute-start | bytes 122888 | tf_op jit(solution)/shard_map/ppermute | solution.py:31
  31.5 1.3 %all-to-all-done.1 = bf16[4,4,8,2560]{3,1,2,0:T(4,128)(2,1)S(1)} async-done(((bf16[4,4,8,2560]{3,1,2,0:T(4,128)(2,1)}), bf16[4,4,8,2560]{3,1,2,0:T(4,128)(2,1)S(1)}, u32[]{:S(2)}, u32[]{:S(2)}) %all-to-all-start.1) | async-done | bytes 655392 | tf_op jit(solution)/shard_map/all_to_all | solution.py:66
  32.7 0.2 copy.40
  33.0 0.1 reshape.80
  33.1 0.4 convolution_convert_fusion
  33.5 0.0 collective-permute-done.3
  33.5 1.3 %collective-permute-done.4 = bf16[4,2,2560]{2,0,1:T(4,128)(2,1)S(1)} collective-permute-done((bf16[4,2,2560]{2,0,1:T(4,128)(2,1)S(1)}, bf16[4,2,2560]{2,0,1:T(4,128)(2,1)S(1)}, u32[]{:S(2)}, u32[]{:S(2)}) %collective-permute-start.4) | collective-permute-done | bytes 40992 | tf_op jit(solution)/shard_map/ppermute | solution.py:31
  34.9 0.1 maximum_maximum_fusion
  35.0 0.2 copy.43
  35.2 1.9 %reshape.81.x_ref = bf16[20,160,128]{2,1,0:T(8,128)(2,1)} reshape(bf16[20,8,2560]{2,1,0:T(8,128)(2,1)S(1)} %copy.43) | data formatting | bytes 1638400 | tf_op jit(solution)/shard_map/reshape | solution.py:217
  37.1 47.4 %shard_map.100 = bf16[2,640,16]{2,1,0:T(8,128)(2,1)} custom-call(bf16[20,160,128]{2,1,0:T(8,128)(2,1)} %reshape.81.x_ref, bf16[16,512]{1,0:T(8,128)(2,1)} %stem_ref.1, bf16[256,512]{1,0:T(8,128)(2,1)} %mem_ref.1, bf16[2,27,32,512]{3,2,1,0:T(8,128)(2,1)} %bitcast.51, f32[2,512]{1,0:T(2,128)} %gain_ref.1, bf16[512,16]{1,0:T(8,128)(2,1)} %copy.44.head_ref), custom_call_target="tpu_custom_call" | custom-call | tf_op jit(solution)/shard_map/pallas_call | solution.py:220
  84.5 1.9 %reshape.83 = bf16[1,2,4,2560]{3,2,1,0:T(4,128)(2,1)} reshape(bf16[2,640,16]{2,1,0:T(8,128)(2,1)} %shard_map.100) | data formatting | bytes 81920 | tf_op jit(solution)/shard_map/reshape | solution.py:236
  (6 shorter events, 0.1 us)
Async XLA Ops:
  0.0 13.8 %copy-start = (bf16[1,2,4,2560]{3,2,1,0:T(4,128)(2,1)S(1)}, bf16[1,2,4,2560]{3,2,1,0:T(4,128)(2,1)}, u32[]{:S(2)}) copy-start(bf16[1,2,4,2560]{3,2,1,0:T(4,128)(2,1)} %param.10) | copy-start | bytes 122884
  0.0 18.2 %copy-start.1 = (bf16[1,2,4,2560]{3,2,1,0:T(4,128)(2,1)S(1)}, bf16[1,2,4,2560]{3,2,1,0:T(4,128)(2,1)}, u32[]{:S(2)}) copy-start(bf16[1,2,4,2560]{3,2,1,0:T(4,128)(2,1)} %param.11) | copy-start | bytes 122884
  2.3 16.0 %all-to-all-start = ((s32[4,1,4]{2,1,0:T(1,128)}), s32[4,1,4]{2,1,0:T(1,128)S(1)}, u32[]{:S(2)}, u32[]{:S(2)}) async-start(s32[4,1,4]{2,1,0:T(1,128)} %bitcast.6), calls=%async_computation | async-start | bytes 4096 | tf_op jit(solution)/shard_map/all_to_all | solution.py:62
  7.8 11.7 %collective-permute-start = (bf16[32,2,2560]{2,0,1:T(8,128)(2,1)S(1)}, bf16[32,2,2560]{2,0,1:T(8,128)(2,1)S(1)}, u32[]{:S(2)}, u32[]{:S(2)}) collective-permute-start(bf16[32,2,2560]{2,0,1:T(8,128)(2,1)S(1)} %get-tuple-element.5), channel_id=1, source_target_pairs={{0,1},{1,2},{2,3},{3,4},{4,5},{5,6},{6,7},{8,9},{9,10},{10,11},{11... | collective-permute-start | bytes 983048 | tf_op jit(solution)/shard_map/ppermute | solution.py:28
  11.9 8.4 %collective-permute-start.1 = (bf16[32,2,2560]{2,0,1:T(8,128)(2,1)S(1)}, bf16[32,2,2560]{2,0,1:T(8,128)(2,1)S(1)}, u32[]{:S(2)}, u32[]{:S(2)}) collective-permute-start(bf16[32,2,2560]{2,0,1:T(8,128)(2,1)S(1)} %get-tuple-element.6), channel_id=1, source_target_pairs={{1,0},{2,1},{3,2},{4,3},{5,4},{6,5},{7,6},{9,8},{10,9},{11,10},{12... | collective-permute-start | bytes 983048 | tf_op jit(solution)/shard_map/ppermute | solution.py:31
  13.9 12.7 %collective-permute-start.2 = (bf16[2,4,2560]{2,0,1:T(2,128)(2,1)S(1)}, bf16[2,4,2560]{2,0,1:T(2,128)(2,1)S(1)}, u32[]{:S(2)}, u32[]{:S(2)}) collective-permute-start(bf16[2,4,2560]{2,0,1:T(2,128)(2,1)S(1)} %bitcast.53), channel_id=1, source_target_pairs={{0,8},{8,16},{16,24},{1,9},{9,17},{17,25},{2,10},{10,18},{18,26},{... | collective-permute-start | bytes 122888 | tf_op jit(solution)/shard_map/ppermute | solution.py:20
  20.7 5.2 %copy-start.3 = (s32[1,16]{1,0:T(1,128)S(1)}, s32[1,16]{1,0:T(1,128)}, u32[]{:S(2)}) copy-start(s32[1,16]{1,0:T(1,128)} %param.14) | copy-start | bytes 196
  20.7 5.2 %copy-start.2 = (bf16[512,16]{0,1:T(8,128)(2,1)S(1)}, bf16[512,16]{0,1:T(8,128)(2,1)}, u32[]{:S(2)}) copy-start(bf16[512,16]{0,1:T(8,128)(2,1)} %param.19) | copy-start | bytes 49156
  21.9 10.8 %all-to-all-start.1 = ((bf16[4,4,8,2560]{3,1,2,0:T(4,128)(2,1)}), bf16[4,4,8,2560]{3,1,2,0:T(4,128)(2,1)S(1)}, u32[]{:S(2)}, u32[]{:S(2)}) async-start(bf16[4,4,8,2560]{3,1,2,0:T(4,128)(2,1)} %copy.39), calls=%async_computation.1 | async-start | bytes 1310720 | tf_op jit(solution)/shard_map/all_to_all | solution.py:66
  26.7 6.8 %collective-permute-start.3 = (bf16[4,2,2560]{2,0,1:T(4,128)(2,1)S(1)}, bf16[4,2,2560]{2,0,1:T(4,128)(2,1)S(1)}, u32[]{:S(2)}, u32[]{:S(2)}) collective-permute-start(bf16[4,2,2560]{2,0,1:T(4,128)(2,1)S(1)} %get-tuple-element.7), channel_id=1, source_target_pairs={{0,1},{1,2},{2,3},{3,4},{4,5},{5,6},{6,7},{8,9},{9,10},{10,11},{11... | collective-permute-start | bytes 122888 | tf_op jit(solution)/shard_map/ppermute | solution.py:28
  29.5 5.3 %collective-permute-start.4 = (bf16[4,2,2560]{2,0,1:T(4,128)(2,1)S(1)}, bf16[4,2,2560]{2,0,1:T(4,128)(2,1)S(1)}, u32[]{:S(2)}, u32[]{:S(2)}) collective-permute-start(bf16[4,2,2560]{2,0,1:T(4,128)(2,1)S(1)} %get-tuple-element.8), channel_id=1, source_target_pairs={{1,0},{2,1},{3,2},{4,3},{5,4},{6,5},{7,6},{9,8},{10,9},{11,10},{12... | collective-permute-start | bytes 122888 | tf_op jit(solution)/shard_map/ppermute | solution.py:31
